TPU v7x, 512 devices: a whole 4x4x16 slice. The times are simulated.
512 devices in a mesh: dp: 16 (over z_lo, x), panel: 32 (over y, z_hi, core).
Axes of the slice: x: 4, y: 4, z: 16 (z_hi: 4, z_lo: 4; z = z_hi * 4 + z_lo), core: 2. Of those that a mesh axis runs over, the one named last changes fastest.
Arguments:
- features: bfloat16 [12288, 4096], P('dp', 'panel'), may hold values from -48 to 48
- sketch: float32 [32, 128, 256], P('panel', 'dp'), may hold values from -6 to 6
- counts: int32 [16], replicated, may hold values from 384 to 768, as said below
Outputs:
- covariance: float32 [4096, 16, 256], P('panel', 'dp')
- basis: float32 [32, 128, 256], P('panel', 'dp')
Inputs may be any that keep to these rules, and one draw needn't show every extreme that they name: `counts`: some dp index has all 768 rows live.
All inputs are finite; a program needn't handle non-finite values.
Results may differ from a plain program's by a relative error of at most 0.0003.
Values may be sent and summed in bfloat16 or wider, within the bound.
No kernel may reach another device: no remote copies, remote signals or barrier semaphores. Data moves between devices by JAX's collectives and lax.ppermute only.
A program may use at most 64 MiB of HBM per device.

v0:
```python
import math
import jax
import jax.numpy as jnp
from jax import lax
from jax.sharding import PartitionSpec as P

ITERS = 2


def local(features, sketch, counts):
    dp_count = lax.axis_size("dp")
    panel_count = lax.axis_size("panel")
    tok_rows, feat_width = features.shape
    sub_rows = sketch.shape[1]
    rank_cols = sketch.shape[2]
    total_width = feat_width * panel_count
    limit = counts[lax.axis_index("dp")]
    live_rows = (lax.iota(jnp.int32, tok_rows) < limit).astype(jnp.bfloat16)
    masked = features * live_rows[:, None]
    token_total = jnp.sum(counts).astype(jnp.float32)
    contract = (((0,), (0,)), ((), ()))
    partial_value = lax.dot_general(
        masked,
        lax.all_gather(features, "panel", axis=1, tiled=True),
        contract,
        preferred_element_type=jnp.float32,
    )
    partial_value = partial_value.reshape(feat_width, panel_count, dp_count, sub_rows)
    partial_value = jnp.transpose(partial_value, (0, 2, 1, 3)).reshape(
        feat_width, dp_count, panel_count * sub_rows
    )
    summed = lax.psum_scatter(partial_value, "dp", scatter_dimension=1, tiled=True)
    covariance = summed / token_total
    cov_flat = covariance.reshape(feat_width, panel_count * sub_rows)
    basis_now = sketch[0]
    for sweep in range(ITERS):
        shaped = jnp.dot(
            cov_flat,
            lax.all_gather(basis_now, "panel", axis=0, tiled=True),
            precision=lax.Precision.HIGHEST,
            preferred_element_type=jnp.float32,
        ).reshape(dp_count, sub_rows, rank_cols)
        basis_block = lax.psum_scatter(shaped, "dp", scatter_dimension=0, tiled=True)[0]
        inner_gram = jnp.dot(
            basis_block.T,
            basis_block,
            precision=lax.Precision.HIGHEST,
            preferred_element_type=jnp.float32,
        )
        summed_gram = lax.psum(inner_gram, ("dp", "panel"))
        factor_low = jnp.linalg.cholesky(summed_gram)
        basis_now = jax.scipy.linalg.solve_triangular(factor_low, basis_block.T, lower=True).T
    scaled = (math.sqrt(total_width) * basis_now)[None]
    return (covariance, scaled)


def solution(mesh):
    in_specs = (P("dp", "panel"), P("panel", "dp", None), P())
    out_specs = (P("panel", "dp", None), P("panel", "dp", None))
    return jax.shard_map(local, mesh=mesh, in_specs=in_specs, out_specs=out_specs, check_vma=False)
```

profile of v0, /device:TPU:4, one launch (start us, length us, event | category | flops | bytes accessed | tf_op | source)
XLA Modules:
  0.0 1509.2 jit_solution(8885281473320648278)
XLA Ops:
  7.2 0.0 all-gather.3.cloned.1.call-start
  7.2 0.7 all-gather.3.cloned.1.call-update
  7.9 0.0 reduce-scatter.4.cloned.1.call-start
  7.9 1.2 dynamic_slice.3
  9.2 0.6 fusion.34
  9.9 128.8 %all-gather.3.cloned.1.call-done = bf16[768,4096]{1,0:T(8,128)(2,1)} async-done(((bf16[768,128]{1,0:T(8,128)(2,1)}), bf16[768,4096]{1,0:T(8,128)(2,1)}) %all-gather.3.cloned.1.call-update) | async-done | bytes 6291472 | tf_op jit(solution)/shard_map/all_gather | solution.py:24
  138.7 5.6 fusion.6
  144.4 1.6 copy.31
  146.0 0.0 reduce-scatter.6.cloned.1.call-start
  146.0 0.6 reduce_sum.9
  147.3 49.7 %all-gather = f32[1,256,256]{2,1,0:T(8,128)S(1)} all-gather(f32[1,8,256]{2,1,0:T(8,128)S(1)} %copy-done), channel_id=2, replica_groups=mesh['dp'=16,'panel'=32] {'panel'}, dimensions={1}, use_global_device_ids=true | all-gather | bytes 270336 | tf_op jit(solution)/shard_map/all_gather | solution.py:39
  197.0 31.1 %reduce-scatter.4.cloned.1.call-done = f32[128,1,256]{0,2,1:T(8,128)} async-done(((f32[128,16,256]{0,2,1:T(8,128)}), f32[128,1,256]{0,2,1:T(8,128)}) %reduce-scatter.4.cloned.1.call-update) | async-done | bytes 131088 | tf_op jit(solution)/shard_map/reduce_scatter | solution.py:32
  228.1 0.9 broadcast_divide_fusion
  229.1 0.1 copy.21
  229.2 0.9 fusion.4
  230.1 0.0 all-reduce.4.cloned.1.call-start
  230.2 86.6 %reduce-scatter.6.cloned.1.call-done = f32[1,8,256]{2,1,0:T(8,128)} async-done(((f32[16,8,256]{2,1,0:T(8,128)}), f32[1,8,256]{2,1,0:T(8,128)}) %reduce-scatter.6.cloned.1.call-update) | async-done | bytes 8208 | tf_op jit(solution)/shard_map/reduce_scatter | solution.py:43
  316.7 1.9 fusion.30
  318.7 0.2 reduce-scatter.8.cloned.1.call-start
  318.9 462.3 %all-reduce.4.cloned.1.call-done = f32[256,256]{0,1:T(8,128)} async-done(((f32[256,256]{0,1:T(8,128)}), f32[256,256]{0,1:T(8,128)}) %all-reduce.4.cloned.1.call-update) | async-done | bytes 262160 | tf_op jit(solution)/shard_map/psum | solution.py:50
  781.2 1.1 copy.23
  782.3 1.0 fusion.3
  783.3 11.7 cholesky.130
  795.1 9.8 custom-call.13
  804.9 0.2 constant_dynamic-update-slice_fusion.3
  805.1 0.3 convolution_subtract_fusion.1
  805.4 11.7 cholesky.147
  817.1 0.7 compare_reduce_fusion.2
  819.2 0.1 triangular_solve.75
  819.2 4.1 while.4
  819.3 0.7 fusion.48
  819.9 1.3 bitcast_dynamic-update-slice_fusion.4
  821.3 0.7 fusion.48
  822.0 1.3 bitcast_dynamic-update-slice_fusion.4
  823.3 19.7 %custom-call.14 = f32[2,128,128]{1,2,0:T(8,128)S(1)} custom-call(f32[2,128,128]{2,1,0:T(8,128)S(1)} %get-tuple-element.18), custom_call_target="InvertDiagBlocksLowerTriangular" | custom-call | tf_op jit(solution)/shard_map/jit(_solve_triangular)/triangular_solve | solution.py:52
  843.0 0.8 fusion.18
  843.8 0.9 convolution_subtract_fusion.3
  844.7 0.2 fusion.17
  844.9 51.6 %all_gather.11 = f32[256,256]{1,0:T(8,128)S(1)} all-gather(f32[8,256]{1,0:T(8,128)S(1)} %maximum_bitcast_fusion), channel_id=1, replica_groups=mesh['dp'=16,'panel'=32] {'panel'}, dimensions={0}, use_global_device_ids=true | all-gather | bytes 270336 | tf_op jit(solution)/shard_map/all_gather | solution.py:39
  896.5 0.9 fusion.1
  897.5 0.3 all-reduce.6.cloned.1.call-start
  897.7 75.2 %reduce-scatter.8.cloned.1.call-done = f32[1,8,256]{2,1,0:T(8,128)} async-done(((f32[16,8,256]{2,1,0:T(8,128)}), f32[1,8,256]{2,1,0:T(8,128)}) %reduce-scatter.8.cloned.1.call-update) | async-done | bytes 8208 | tf_op jit(solution)/shard_map/reduce_scatter | solution.py:43
  972.9 1.9 fusion.28
  974.9 0.8 copy.26
  975.6 461.6 %all-reduce.6.cloned.1.call-done = f32[256,256]{0,1:T(8,128)} async-done(((f32[256,256]{0,1:T(8,128)}), f32[256,256]{0,1:T(8,128)}) %all-reduce.6.cloned.1.call-update) | async-done | bytes 262160 | tf_op jit(solution)/shard_map/psum | solution.py:50
  1437.3 1.1 copy.25
  1438.3 1.0 fusion
  1439.3 11.7 cholesky.164
  1451.1 9.8 custom-call.15
  1460.9 0.2 constant_dynamic-update-slice_fusion.1
  1461.1 0.3 convolution_subtract_fusion
  1461.4 11.7 cholesky.181
  1473.2 0.6 compare_reduce_fusion
  1473.8 0.7 compare_reduce_fusion.1
  1475.8 4.3 while.5
  1476.1 0.7 fusion.49
  1476.8 1.3 bitcast_dynamic-update-slice_fusion.5
  1478.1 0.7 fusion.49
  1478.8 1.3 bitcast_dynamic-update-slice_fusion.5
  1480.2 19.7 %custom-call.16 = f32[2,128,128]{1,2,0:T(8,128)S(1)} custom-call(f32[2,128,128]{2,1,0:T(8,128)S(1)} %get-tuple-element.19), custom_call_target="InvertDiagBlocksLowerTriangular" | custom-call | tf_op jit(solution)/shard_map/jit(_solve_triangular)/triangular_solve | solution.py:52
  1499.8 0.8 fusion.13
  1500.7 0.9 convolution_subtract_fusion.2
  1501.5 0.2 fusion.12
  1501.7 0.6 fusion.27
  (27 shorter events, 0.4 us)
Async XLA Ops:
  7.2 131.6 %all-gather.3.cloned.1.call-start = ((), (), s32[]{:S(2)}) async-start(), calls=%async_computation.3 | async-start | bytes 6488064 | tf_op jit(solution)/shard_map/all_gather | solution.py:24
  7.9 220.2 %reduce-scatter.4.cloned.1.call-start = ((), (), s32[]{:S(2)}) async-start(), calls=%async_computation.4 | async-start | bytes 2228224 | tf_op jit(solution)/shard_map/reduce_scatter | solution.py:32
  9.8 136.2 %copy-start.1 = (s32[16]{0:T(128)S(1)}, s32[16]{0:T(128)}, u32[]{:S(2)}) copy-start(s32[16]{0:T(128)} %param.8) | copy-start | bytes 196
  9.9 137.4 %copy-start = (f32[1,8,256]{2,1,0:T(8,128)S(1)}, f32[1,8,256]{2,1,0:T(8,128)}, u32[]{:S(2)}) copy-start(f32[1,8,256]{2,1,0:T(8,128)} %param.7) | copy-start | bytes 24580
  146.0 170.8 %reduce-scatter.6.cloned.1.call-start = ((), (), s32[]{:S(2)}) async-start(), calls=%async_computation.5 | async-start | bytes 139264 | tf_op jit(solution)/shard_map/reduce_scatter | solution.py:43
  230.1 551.1 %all-reduce.4.cloned.1.call-start = ((), (), s32[]{:S(2)}) async-start(), calls=%async_computation.6 | async-start | bytes 524288 | tf_op jit(solution)/shard_map/psum | solution.py:50
  318.7 654.3 %reduce-scatter.8.cloned.1.call-start = ((), (), s32[]{:S(2)}) async-start(), calls=%async_computation.7 | async-start | bytes 139264 | tf_op jit(solution)/shard_map/reduce_scatter | solution.py:43
  897.5 539.8 %all-reduce.6.cloned.1.call-start = ((), (), s32[]{:S(2)}) async-start(), calls=%async_computation.8 | async-start | bytes 524288 | tf_op jit(solution)/shard_map/psum | solution.py:50
Sparse Core Ops, SparseCore 0:
  11.1 127.6 all-gather.2
  146.1 82.0 reduce-scatter.3
  231.5 85.1 reduce-scatter.5
  322.9 458.2 all-reduce.3
  897.6 75.3 reduce-scatter.7
  979.1 458.0 all-reduce.5
where the time goes:
time: 1510 us
  waiting for transfers between devices  1250 us (83%)
  other arithmetic  113 us (7%)
  blocking collectives  101 us (7%)
  between operations  17.5 us (1%)
  matrix products  16.1 us (1%)
    psum x2, waiting for transfers between devices, local(): summed_gram = lax.psum(inner_gram, ('dp', 'panel'))  924 us
    reduce_scatter x2, waiting for transfers between devices, local(): lax.psum_scatter(shaped, 'dp', scatter_dimension=0, tiled=True)[0]  162 us
    all_gather x1, waiting for transfers between devices, local(): lax.all_gather(features, 'panel', axis=1, tiled=True)  129 us
    all_gather x2, blocking collectives, local(): lax.all_gather(basis_now, 'panel', axis=0, tiled=True)  101 us
    another operation x13, other arithmetic, local(): factor_low = jnp.linalg.cholesky(summed_gram)  68.7 us
    another operation x5, other arithmetic, local(): jax.scipy.linalg.solve_triangular(factor_low, basis_block.T, lower=True)  39.4 us
    reduce_scatter x1, waiting for transfers between devices, local(): lax.psum_scatter(partial_value, 'dp', scatter_dimension=1, tiled=True)  31.1 us
  transfers between devices with their start and end apart: 6, of which 6 were waited for; matrix products, arithmetic and copies ran while one was open for 0% of the time, Pallas kernels for 0%

commit v1 on v0

--- a/solution.py
+++ b/solution.py
@@ -47,7 +47,8 @@
             precision=lax.Precision.HIGHEST,
             preferred_element_type=jnp.float32,
         )
-        summed_gram = lax.psum(inner_gram, ("dp", "panel"))
+        one_axis = lax.psum(inner_gram, "panel")
+        summed_gram = lax.psum(one_axis, "dp")
         factor_low = jnp.linalg.cholesky(summed_gram)
         basis_now = jax.scipy.linalg.solve_triangular(factor_low, basis_block.T, lower=True).T
     scaled = (math.sqrt(total_width) * basis_now)[None]

time: 1510 us -> 1610 us (1.066)
  the two profiles are of different devices: /device:TPU:4 before, /device:TPU:8 now
where the time goes in v1:
time: 1610 us
  waiting for transfers between devices  1350 us (84%)
  other arithmetic  113 us (7%)
  blocking collectives  96.7 us (6%)
  between operations  17.5 us (1%)
  matrix products  16.1 us (1%)
    psum x2, waiting for transfers between devices, local(): one_axis = lax.psum(inner_gram, 'panel')  653 us
    psum x2, waiting for transfers between devices, local(): summed_gram = lax.psum(one_axis, 'dp')  362 us
    reduce_scatter x2, waiting for transfers between devices, local(): lax.psum_scatter(shaped, 'dp', scatter_dimension=0, tiled=True)[0]  171 us
    all_gather x1, waiting for transfers between devices, local(): lax.all_gather(features, 'panel', axis=1, tiled=True)  129 us
    all_gather x2, blocking collectives, local(): lax.all_gather(basis_now, 'panel', axis=0, tiled=True)  96.7 us
    another operation x13, other arithmetic, local(): factor_low = jnp.linalg.cholesky(summed_gram)  68.7 us
    another operation x5, other arithmetic, local(): jax.scipy.linalg.solve_triangular(factor_low, basis_block.T, lower=True)  39.4 us
    reduce_scatter x1, waiting for transfers between devices, local(): lax.psum_scatter(partial_value, 'dp', scatter_dimension=1, tiled=True)  39 us
  transfers between devices with their start and end apart: 8, of which 8 were waited for; matrix products, arithmetic and copies ran while one was open for 0% of the time, Pallas kernels for 0%

profile of v1, /device:TPU:8, one launch (start us, length us, event | category | flops | bytes accessed | tf_op | source)
XLA Modules:
  0.0 1612.7 jit_solution(17695246071949664032)
XLA Ops:
  7.2 0.7 all-gather.3.cloned.1.call-update
  7.9 1.2 dynamic_slice.3
  9.2 0.6 fusion.34
  9.9 128.8 %all-gather.3.cloned.1.call-done = bf16[768,4096]{1,0:T(8,128)(2,1)} async-done(((bf16[768,128]{1,0:T(8,128)(2,1)}), bf16[768,4096]{1,0:T(8,128)(2,1)}) %all-gather.3.cloned.1.call-update) | async-done | bytes 6291472 | tf_op jit(solution)/shard_map/all_gather | solution.py:24
  138.7 5.6 fusion.6
  144.3 1.6 copy.31
  145.9 0.0 reduce-scatter.6.cloned.1.call-start
  146.0 0.6 reduce_sum.9
  147.3 46.7 %all-gather = f32[1,256,256]{2,1,0:T(8,128)S(1)} all-gather(f32[1,8,256]{2,1,0:T(8,128)S(1)} %copy-done), channel_id=2, replica_groups=mesh['dp'=16,'panel'=32] {'panel'}, dimensions={1}, use_global_device_ids=true | all-gather | bytes 270336 | tf_op jit(solution)/shard_map/all_gather | solution.py:39
  194.0 39.0 %reduce-scatter.4.cloned.1.call-done = f32[128,1,256]{0,2,1:T(8,128)} async-done(((f32[128,16,256]{0,2,1:T(8,128)}), f32[128,1,256]{0,2,1:T(8,128)}) %reduce-scatter.4.cloned.1.call-update) | async-done | bytes 131088 | tf_op jit(solution)/shard_map/reduce_scatter | solution.py:32
  233.0 0.9 broadcast_divide_fusion
  233.9 0.1 copy.21
  234.0 0.9 fusion.4
  235.0 0.0 all-reduce.6.cloned.1.call-start
  235.0 86.3 %reduce-scatter.6.cloned.1.call-done = f32[1,8,256]{2,1,0:T(8,128)} async-done(((f32[16,8,256]{2,1,0:T(8,128)}), f32[1,8,256]{2,1,0:T(8,128)}) %reduce-scatter.6.cloned.1.call-update) | async-done | bytes 8208 | tf_op jit(solution)/shard_map/reduce_scatter | solution.py:43
  321.3 1.9 fusion.30
  323.3 326.7 %all-reduce.6.cloned.1.call-done = f32[256,256]{0,1:T(8,128)} async-done(((f32[256,256]{0,1:T(8,128)}), f32[256,256]{0,1:T(8,128)}) %all-reduce.6.cloned.1.call-update) | async-done | bytes 262160 | tf_op jit(solution)/shard_map/psum | solution.py:50
  650.1 0.2 reduce-scatter.8.cloned.1.call-start
  650.3 181.0 %all-reduce.8.cloned.1.call-done = f32[256,256]{0,1:T(8,128)} async-done(((f32[256,256]{0,1:T(8,128)}), f32[256,256]{0,1:T(8,128)}) %all-reduce.8.cloned.1.call-update) | async-done | bytes 262160 | tf_op jit(solution)/shard_map/psum | solution.py:51
  831.3 1.1 copy.23
  832.4 1.0 fusion.3
  833.4 11.7 cholesky.130
  845.1 9.8 custom-call.13
  854.9 0.2 constant_dynamic-update-slice_fusion.3
  855.2 0.3 convolution_subtract_fusion.1
  855.4 11.7 cholesky.147
  867.2 0.7 compare_reduce_fusion.2
  869.2 0.1 triangular_solve.75
  869.3 4.3 while.4
  869.5 0.7 fusion.48
  870.2 1.3 bitcast_dynamic-update-slice_fusion.4
  871.6 0.7 fusion.48
  872.2 1.3 bitcast_dynamic-update-slice_fusion.4
  873.6 19.7 %custom-call.14 = f32[2,128,128]{1,2,0:T(8,128)S(1)} custom-call(f32[2,128,128]{2,1,0:T(8,128)S(1)} %get-tuple-element.18), custom_call_target="InvertDiagBlocksLowerTriangular" | custom-call | tf_op jit(solution)/shard_map/jit(_solve_triangular)/triangular_solve | solution.py:53
  893.3 0.8 fusion.18
  894.1 0.9 convolution_subtract_fusion.3
  895.0 0.2 fusion.17
  895.2 50.0 %all_gather.11 = f32[256,256]{1,0:T(8,128)S(1)} all-gather(f32[8,256]{1,0:T(8,128)S(1)} %maximum_bitcast_fusion), channel_id=1, replica_groups=mesh['dp'=16,'panel'=32] {'panel'}, dimensions={0}, use_global_device_ids=true | all-gather | bytes 270336 | tf_op jit(solution)/shard_map/all_gather | solution.py:39
  945.1 0.9 fusion.1
  946.2 84.5 %reduce-scatter.8.cloned.1.call-done = f32[1,8,256]{2,1,0:T(8,128)} async-done(((f32[16,8,256]{2,1,0:T(8,128)}), f32[1,8,256]{2,1,0:T(8,128)}) %reduce-scatter.8.cloned.1.call-update) | async-done | bytes 8208 | tf_op jit(solution)/shard_map/reduce_scatter | solution.py:43
  1030.6 1.9 fusion.28
  1032.5 0.0 all-reduce.12.cloned.1.call-start
  1032.6 326.5 %all-reduce.10.cloned.1.call-done = f32[256,256]{0,1:T(8,128)} async-done(((f32[256,256]{0,1:T(8,128)}), f32[256,256]{0,1:T(8,128)}) %all-reduce.10.cloned.1.call-update) | async-done | bytes 262160 | tf_op jit(solution)/shard_map/psum | solution.py:50
  1359.1 0.8 copy.26
  1359.9 180.8 %all-reduce.12.cloned.1.call-done = f32[256,256]{0,1:T(8,128)} async-done(((f32[256,256]{0,1:T(8,128)}), f32[256,256]{0,1:T(8,128)}) %all-reduce.12.cloned.1.call-update) | async-done | bytes 262160 | tf_op jit(solution)/shard_map/psum | solution.py:51
  1540.7 1.1 copy.25
  1541.8 1.0 fusion
  1542.8 11.7 cholesky.164
  1554.6 9.8 custom-call.15
  1564.4 0.2 constant_dynamic-update-slice_fusion.1
  1564.6 0.3 convolution_subtract_fusion
  1564.9 11.7 cholesky.181
  1576.6 0.6 compare_reduce_fusion
  1577.3 0.7 compare_reduce_fusion.1
  1579.3 4.3 while.5
  1579.6 0.7 fusion.49
  1580.3 1.3 bitcast_dynamic-update-slice_fusion.5
  1581.6 0.7 fusion.49
  1582.3 1.3 bitcast_dynamic-update-slice_fusion.5
  1583.6 19.7 %custom-call.16 = f32[2,128,128]{1,2,0:T(8,128)S(1)} custom-call(f32[2,128,128]{2,1,0:T(8,128)S(1)} %get-tuple-element.19), custom_call_target="InvertDiagBlocksLowerTriangular" | custom-call | tf_op jit(solution)/shard_map/jit(_solve_triangular)/triangular_solve | solution.py:53
  1603.3 0.8 fusion.13
  1604.2 0.9 convolution_subtract_fusion.2
  1605.0 0.2 fusion.12
  1605.2 0.6 fusion.27
  (33 shorter events, 0.6 us)
Async XLA Ops:
  7.2 131.5 %all-gather.3.cloned.1.call-start = ((), (), s32[]{:S(2)}) async-start(), calls=%async_computation.3 | async-start | bytes 6488064 | tf_op jit(solution)/shard_map/all_gather | solution.py:24
  7.9 225.1 %reduce-scatter.4.cloned.1.call-start = ((), (), s32[]{:S(2)}) async-start(), calls=%async_computation.4 | async-start | bytes 2228224 | tf_op jit(solution)/shard_map/reduce_scatter | solution.py:32
  9.8 136.1 %copy-start.1 = (s32[16]{0:T(128)S(1)}, s32[16]{0:T(128)}, u32[]{:S(2)}) copy-start(s32[16]{0:T(128)} %param.8) | copy-start | bytes 196
  9.9 137.4 %copy-start = (f32[1,8,256]{2,1,0:T(8,128)S(1)}, f32[1,8,256]{2,1,0:T(8,128)}, u32[]{:S(2)}) copy-start(f32[1,8,256]{2,1,0:T(8,128)} %param.7) | copy-start | bytes 24580
  145.9 175.4 %reduce-scatter.6.cloned.1.call-start = ((), (), s32[]{:S(2)}) async-start(), calls=%async_computation.5 | async-start | bytes 139264 | tf_op jit(solution)/shard_map/reduce_scatter | solution.py:43
  235.0 415.1 %all-reduce.6.cloned.1.call-start = ((), (), s32[]{:S(2)}) async-start(), calls=%async_computation.6 | async-start | bytes 524288 | tf_op jit(solution)/shard_map/psum | solution.py:50
  323.2 508.0 %all-reduce.8.cloned.1.call-start = ((), (), s32[]{:S(2)}) async-start(), calls=%async_computation.7 | async-start | bytes 524288 | tf_op jit(solution)/shard_map/psum | solution.py:51
  650.1 380.6 %reduce-scatter.8.cloned.1.call-start = ((), (), s32[]{:S(2)}) async-start(), calls=%async_computation.8 | async-start | bytes 139264 | tf_op jit(solution)/shard_map/reduce_scatter | solution.py:43
  946.1 413.0 %all-reduce.10.cloned.1.call-start = ((), (), s32[]{:S(2)}) async-start(), calls=%async_computation.9 | async-start | bytes 524288 | tf_op jit(solution)/shard_map/psum | solution.py:50
  1032.5 508.2 %all-reduce.12.cloned.1.call-start = ((), (), s32[]{:S(2)}) async-start(), calls=%async_computation.10 | async-start | bytes 524288 | tf_op jit(solution)/shard_map/psum | solution.py:51
Sparse Core Ops, SparseCore 0:
  11.1 127.5 all-gather.2
  146.0 86.9 reduce-scatter.3
  236.4 84.9 reduce-scatter.5
  324.3 325.6 all-reduce.5
  652.8 178.4 all-reduce.7
  946.2 84.3 reduce-scatter.7
  1033.5 325.5 all-reduce.9
  1362.3 178.4 all-reduce.11
